TPU v7x, 768 devices: a whole 4x8x12 slice. The times are simulated.
768 devices in a mesh: blk: 32 (over z_hi, y, core), uly: 24 (over x, z_lo).
Axes of the slice: x: 4, y: 8, z: 12 (z_hi: 2, z_lo: 6; z = z_hi * 6 + z_lo), core: 2. Of those that a mesh axis runs over, the one named last changes fastest.
Arguments:
- qkv: bfloat16 [49152, 3, 3072], P(('blk', 'uly')), may hold values from -9 to 9
Outputs:
- attended: float32 [49152, 3072], P('blk', 'uly')
- log_total: float32 [24, 49152], P('uly', 'blk')
All inputs are finite; a program needn't handle non-finite values.
Results may differ from a plain program's by a relative error of at most 0.0027.
Values may be sent and summed in bfloat16 or wider, within the bound.
A program may use at most 32 MiB of HBM per device.

v0:
```python
import math

import jax
import jax.numpy as jnp
from jax import lax
from jax.sharding import PartitionSpec as P

HEAD_DIM = 128


def from_behind(value, axis, steps):
    count = lax.axis_size(axis)
    pairs = [(source, (source + steps) % count) for source in range(count)]
    return lax.ppermute(value, axis, pairs)


def block_scores(query_rows, key_rows, temper):
    return (
        jnp.einsum("rhd,khd->hrk", query_rows, key_rows, preferred_element_type=jnp.float32)
        * temper
    )


def attend_first(query_rows, key_rows, value_rows, temper):
    scores = block_scores(query_rows, key_rows, temper)
    top = jnp.max(scores, axis=2)
    weights = jnp.exp(scores - top[:, :, None])
    total = jnp.sum(weights, axis=2)
    accum = jnp.einsum(
        "hrk,khd->hrd", weights.astype(jnp.bfloat16), value_rows, preferred_element_type=jnp.float32
    )
    return (top, total, accum)


def attend_next(running, query_rows, key_rows, value_rows, temper):
    top, total, accum = running
    scores = block_scores(query_rows, key_rows, temper)
    newtop = jnp.maximum(top, jnp.max(scores, axis=2))
    factor = jnp.exp(top - newtop)
    weights = jnp.exp(scores - newtop[:, :, None])
    total = total * factor + jnp.sum(weights, axis=2)
    accum = accum * factor[:, :, None] + jnp.einsum(
        "hrk,khd->hrd", weights.astype(jnp.bfloat16), value_rows, preferred_element_type=jnp.float32
    )
    return (newtop, total, accum)


def shards(qkv):
    width = qkv.shape[2] // lax.axis_size("uly")
    heads_local = width // HEAD_DIM
    temper = 1.0 / math.sqrt(HEAD_DIM)
    grouped = lax.all_to_all(qkv, "uly", split_axis=2, concat_axis=0, tiled=True)
    prev_pairs = from_behind(grouped[:, 1:], "blk", 1)
    block_len = grouped.shape[0]
    row_count = math.gcd(block_len, 512)
    queries = grouped[:, 0].reshape(block_len // row_count, row_count, heads_local, HEAD_DIM)
    own_keys = grouped[:, 1].reshape(block_len, heads_local, HEAD_DIM)
    own_values = grouped[:, 2].reshape(block_len, heads_local, HEAD_DIM)
    prev_keys = prev_pairs[:, 0].reshape(block_len, heads_local, HEAD_DIM)
    prev_values = prev_pairs[:, 1].reshape(block_len, heads_local, HEAD_DIM)

    def per_rows(query_rows):
        running = attend_first(query_rows, own_keys, own_values, temper)
        top, total, accum = attend_next(running, query_rows, prev_keys, prev_values, temper)
        normed = accum / total[:, :, None]
        return (jnp.transpose(normed, (1, 0, 2)).reshape(row_count, width), top + jnp.log(total))

    attended_rows, log_rows = lax.map(per_rows, queries)
    attended = attended_rows.reshape(block_len, width)
    log_total = jnp.transpose(log_rows, (1, 0, 2)).reshape(heads_local, block_len)
    return (attended, log_total)


def solution(mesh):
    placed = (P(("blk", "uly"), None, None),)
    return jax.shard_map(
        shards,
        mesh=mesh,
        in_specs=placed,
        out_specs=(P("blk", "uly"), P("uly", "blk")),
        check_vma=False,
    )
```

profile of v0, /device:TPU:64, one launch (start us, length us, event | category | flops | bytes accessed | tf_op | source)
XLA Modules:
  0.0 126.7 jit_solution(12636970682460005458)
XLA Ops:
  0.6 4.6 %copy.5 = bf16[64,3,3072]{0,1,2:T(4,128)(2,1)S(1)} copy(bf16[64,3,3072]{2,0,1:T(8,128)(2,1)} %param.3) | data formatting | bytes 2359296 | tf_op args[0]
  5.2 3.5 %reshape.141 = bf16[24,2,12288]{2,1,0:T(2,128)(2,1)} reshape(bf16[3072,3,64]{2,1,0:T(4,128)(2,1)S(1)} %bitcast.65) | data formatting | bytes 2359296
  8.7 57.2 %all_to_all.18 = bf16[24,2,12288]{2,1,0:T(2,128)(2,1)} all-to-all(bf16[24,2,12288]{2,1,0:T(2,128)(2,1)} %reshape.141), channel_id=1, replica_groups=mesh['blk'=32,'uly'=24] {'uly'}, dimensions={0} | all-to-all | bytes 2359296 | tf_op jit(solution)/shard_map/all_to_all | solution.py:52
  65.9 4.2 %reshape.142 = bf16[3072,3,64]{2,1,0:T(4,128)(2,1)S(1)} reshape(bf16[24,2,12288]{2,1,0:T(2,128)(2,1)} %all_to_all.18) | data formatting | bytes 2359296
  70.1 3.8 %copy.6 = bf16[24,64,3,128]{3,1,0,2:T(8,128)(2,1)} copy(bf16[24,64,3,128]{1,2,3,0:T(4,128)(2,1)S(1)} %bitcast.64) | data formatting | bytes 2359296 | tf_op jit(solution)/shard_map/all_to_all | solution.py:52
  73.9 1.2 slice.27
  75.1 1.9 %collective-permute-start = (bf16[1536,2,128]{2,0,1:T(8,128)(2,1)S(1)}, bf16[1536,2,128]{2,0,1:T(8,128)(2,1)S(1)}, u32[]{:S(2)}, u32[]{:S(2)}) collective-permute-start(bf16[1536,2,128]{2,0,1:T(8,128)(2,1)S(1)} %slice.27), channel_id=1, source_target_pairs={{0,24},{24,48},{48,72},{72,96},{96,120},{120,144},{144,168},{168,1... | collective-permute-start | bytes 2359304 | tf_op jit(solution)/shard_map/ppermute | solution.py:14
  77.0 1.3 %fusion.37 = (bf16[1536,1,128]{2,0,1:T(8,128)(2,1)S(1)}, bf16[1536,1,128]{2,0,1:T(8,128)(2,1)S(1)}, bf16[1536,1,128]{2,0,1:T(8,128)(2,1)S(1)}) fusion(bf16[1536,3,128]{2,0,1:T(8,128)(2,1)} %bitcast.67), kind=kLoop, calls=%fused_computation.32 | loop fusion | bytes 2359296 | tf_op jit(solution)/shard_map/slice | solution.py:58
  78.3 34.7 %collective-permute-done = bf16[1536,2,128]{2,0,1:T(8,128)(2,1)S(1)} collective-permute-done((bf16[1536,2,128]{2,0,1:T(8,128)(2,1)S(1)}, bf16[1536,2,128]{2,0,1:T(8,128)(2,1)S(1)}, u32[]{:S(2)}, u32[]{:S(2)}) %collective-permute-start) | collective-permute-done | bytes 786464 | tf_op jit(solution)/shard_map/ppermute | solution.py:14
  113.0 0.1 fusion.38
  113.0 12.8 %while.12 = (s32[]{:T(128)}, f32[3,512,128]{2,1,0:T(8,128)S(1)}, f32[3,1,512]{2,1,0:T(1,128)}, bf16[3,512,1,128]{3,1,2,0:T(8,128)(2,1)S(1)}, bf16[1536,1,128]{2,...) while((s32[]{:T(128)}, f32[3,512,128]{2,1,0:T(8,128)S(1)}, ...), condition=%wide.region_5.6_spmd, body=%wide.region_0.5_spmd.sunk | while | flops 814942720 | bytes 21545576 | solution.py:68
  113.1 0.7 fusion.53
  113.7 0.7 fusion.52
  114.4 1.0 fusion.55
  115.4 0.6 add_dynamic-update-slice_fusion.2
  116.0 0.6 fusion.54
  116.7 0.6 fusion.56
  117.3 0.7 fusion.53
  118.0 0.7 fusion.52
  118.6 1.0 fusion.55
  119.7 0.6 add_dynamic-update-slice_fusion.2
  120.3 0.6 fusion.54
  120.9 0.6 fusion.56
  121.6 0.7 fusion.53
  122.2 0.7 fusion.52
  122.9 1.0 fusion.55
  123.9 0.6 add_dynamic-update-slice_fusion.2
  124.5 0.6 fusion.54
  125.2 0.6 fusion.56
  125.9 0.0 copy-start
  125.9 0.9 copy-done
  (8 shorter events, 0.0 us)
Async XLA Ops:
  75.1 37.9 %collective-permute-start = (bf16[1536,2,128]{2,0,1:T(8,128)(2,1)S(1)}, bf16[1536,2,128]{2,0,1:T(8,128)(2,1)S(1)}, u32[]{:S(2)}, u32[]{:S(2)}) collective-permute-start(bf16[1536,2,128]{2,0,1:T(8,128)(2,1)S(1)} %slice.27), channel_id=1, source_target_pairs={{0,24},{24,48},{48,72},{72,96},{96,120},{120,144},{144,168},{168,1... | collective-permute-start | bytes 2359304 | tf_op jit(solution)/shard_map/ppermute | solution.py:14
  125.9 0.9 copy-start
where the time goes:
time: 127 us
  blocking collectives  57.2 us (45%)
  waiting for transfers between devices  34.7 us (27%)
  local copies, waits for them, and re-layouts  19.4 us (15%)
  matrix products  7.79 us (6%)
  other arithmetic  4.92 us (4%)
  starting transfers between devices  1.92 us (2%)
    all_to_all x1, blocking collectives, shards(): lax.all_to_all(qkv, 'uly', split_axis=2, concat_axis=0, tiled=True)  57.2 us
    ppermute x1, waiting for transfers between devices, from_behind(): return lax.ppermute(value, axis, pairs)  34.7 us
    unnamed x5, local copies, waits for them, and re-layouts  13.1 us
    dot_general x6, matrix products, block_scores(): jnp.einsum('rhd,khd->hrk', query_rows, key_rows, preferred_element_type=j...  3.94 us
    all_to_all x1, local copies, waits for them, and re-layouts, shards(): lax.all_to_all(qkv, 'uly', split_axis=2, concat_axis=0, tiled=True)  3.75 us
    reduce_sum x3, other arithmetic, attend_first(): total = jnp.sum(weights, axis=2)  3.06 us
  transfers between devices with their start and end apart: 1, of which 1 were waited for; matrix products, arithmetic and copies ran while one was open for 1% of the time, Pallas kernels for 0%

commit v1 on v0

v1 whole, which is shorter than its diff:
```python
import functools
import math

import jax
import jax.numpy as jnp
from jax import lax
from jax.experimental import pallas as pl
from jax.experimental.pallas import tpu as pltpu
from jax.sharding import PartitionSpec as P

MESH = pl.DeviceIdType.MESH
HEAD_DIM = 128
N_X, N_Z, N_Y = 4, 6, 8
N_ULY = N_X * N_Z
N_BLK = 32
HALF = N_Z // 2
OWN_SLOT = 1
GROUP = 4
SCALE = math.log2(math.e) / math.sqrt(HEAD_DIM)


def peer(uly, slot, sign):
    x, z = uly // N_Z, lax.rem(uly, N_Z)
    half, place = z // HALF, lax.rem(z, HALF)
    near, turn = lax.rem(slot, 2), slot // 2
    dz, dx = turn // N_X, lax.rem(turn, N_X)
    to_half = jnp.where(near == 1, half, 1 - half)
    to_place = lax.rem(place + sign * dz + HALF, HALF)
    to_x = lax.rem(x + sign * dx + N_X, N_X)
    return to_x * N_Z + to_half * HALF + to_place


def kernel(
    x_ref, o_ref, l_ref, queries, own, prev, stage, top_ref, total_ref,
    loc_sem, q_send, q_recv, kv_send, kv_recv, f_send, f_recv, a_send, a_recv, b_send,
):
    blk, uly = lax.axis_index("blk"), lax.axis_index("uly")
    zhi, y, core = blk // (2 * N_Y), lax.rem(blk // 2, N_Y), lax.rem(blk, 2)
    tokens = x_ref.shape[1]
    following, preceding = lax.rem(blk + 1, N_BLK), lax.rem(blk + N_BLK - 1, N_BLK)
    last = jnp.logical_and(y == N_Y - 1, core == 1)
    first = jnp.logical_and(y == 0, core == 0)
    relay = jnp.logical_and(y != N_Y - 1, core == 1)

    def block_at(zhi_, y_, core_):
        return (zhi_ * N_Y + y_) * 2 + core_

    wrap_source = block_at(zhi, N_Y - 1, 1)
    wrap_target = block_at(1 - zhi, 0, 0)

    barrier = pltpu.get_barrier_semaphore()

    def greet(b, u):
        pl.semaphore_signal(barrier, inc=1, device_id=(b, u), device_id_type=MESH)

    @pl.loop(1, N_ULY)
    def _(k):
        greet(blk, lax.rem(uly + k, N_ULY))

    @pl.when(jnp.logical_not(first))
    def _():
        greet(preceding, uly)

    @pl.when(relay)
    def _():
        greet(wrap_source, uly)

    @pl.when(first)
    def _():
        @pl.loop(0, N_ULY)
        def _(j):
            greet(block_at(1 - zhi, lax.rem(j, N_Y), 1), peer(uly, j, -1))

    pl.semaphore_wait(
        barrier,
        N_ULY - 1 + jnp.where(last, N_Y - 1, 1) + jnp.where(core == 1, N_ULY // N_Y, 0),
    )

    def rows(s):
        return pl.ds(pl.multiple_of(s * tokens, tokens), tokens)

    def head(u):
        return pl.ds(pl.multiple_of(u * HEAD_DIM, HEAD_DIM), HEAD_DIM)

    remote = functools.partial(pltpu.make_async_remote_copy, device_id_type=MESH)

    def send_q(j):
        to = peer(uly, j, 1)
        return remote(
            x_ref.at[0, :, head(to)], queries.at[rows(uly)], q_send.at[j], q_recv.at[j],
            device_id=(blk, to),
        )

    def send_kv(j):
        to = peer(uly, j, 1)
        return remote(
            x_ref.at[1:3, :, head(to)], own.at[:, rows(j)], kv_send.at[j], kv_recv.at[j],
            device_id=(blk, to),
        )

    def forward(j):
        return remote(
            own.at[:, rows(j)], prev.at[:, rows(j)], f_send.at[j], f_recv.at[j],
            device_id=(following, uly),
        )

    def spread(j):
        return remote(
            x_ref.at[1:3, :, head(peer(uly, j, 1))], stage.at[j // N_Y], a_send.at[j],
            a_recv.at[j // N_Y], device_id=(block_at(zhi, lax.rem(j, N_Y), 1), uly),
        )

    def cross_staged(k):
        j = k * N_Y + y
        return remote(
            stage.at[k], prev.at[:, rows(j)], b_send.at[k], f_recv.at[j],
            device_id=(wrap_target, peer(uly, j, 1)),
        )

    def cross_direct(k):
        j = k * N_Y + N_Y - 1
        to = peer(uly, j, 1)
        return remote(
            x_ref.at[1:3, :, head(to)], prev.at[:, rows(j)], b_send.at[k], f_recv.at[j],
            device_id=(wrap_target, to),
        )

    own_q = pltpu.make_async_copy(x_ref.at[0, :, head(uly)], queries.at[rows(uly)], loc_sem.at[0])
    own_kv = pltpu.make_async_copy(
        x_ref.at[1:3, :, head(uly)], own.at[:, rows(OWN_SLOT)], loc_sem.at[1]
    )
    own_q.start()
    own_kv.start()

    @pl.loop(0, N_ULY)
    def _(j):
        @pl.when(j != OWN_SLOT)
        def _():
            send_q(j).start()

        @pl.when(jnp.logical_and(last, lax.rem(j, N_Y) != N_Y - 1))
        def _():
            spread(j).start()

    @pl.when(relay)
    def _():
        @pl.loop(0, N_ULY // N_Y)
        def _(k):
            spread(k * N_Y).wait_recv()
            cross_staged(k).start()

    @pl.when(last)
    def _():
        @pl.loop(0, N_ULY // N_Y)
        def _(k):
            cross_direct(k).start()

    @pl.loop(0, N_ULY)
    def _(j):
        @pl.when(j != OWN_SLOT)
        def _():
            send_kv(j).start()

    own_q.wait()
    own_kv.wait()

    @pl.when(jnp.logical_not(last))
    def _():
        forward(OWN_SLOT).start()

    @pl.loop(0, N_ULY)
    def _(j):
        @pl.when(j != OWN_SLOT)
        def _():
            send_q(j).wait_recv()

    def arrive(g):
        @pl.loop(0, GROUP)
        def _(i):
            j = g * GROUP + i

            @pl.when(j != OWN_SLOT)
            def _():
                send_kv(j).wait_recv()

                @pl.when(jnp.logical_not(last))
                def _():
                    forward(j).start()

    def arrive_prev(g):
        @pl.loop(0, GROUP)
        def _(i):
            forward(g * GROUP + i).wait_recv()

    wide = GROUP * tokens

    def attend(held, g, start):
        span = pl.ds(pl.multiple_of(g * wide, wide), wide)
        scores = lax.dot_general(
            queries[...], held[0, span, :], (((1,), (1,)), ((), ())),
            preferred_element_type=jnp.float32,
        )
        high = jnp.max(scores, axis=1, keepdims=True) * SCALE
        if start:
            new_top = jnp.broadcast_to(high, top_ref.shape)
        else:
            old_top = top_ref[...]
            new_top = jnp.maximum(old_top, high)
            factor = jnp.exp2(old_top - new_top)
        copies = wide // HEAD_DIM
        weights = jnp.exp2(scores * SCALE - jnp.concatenate([new_top] * copies, axis=1))
        part = weights[:, :HEAD_DIM]
        for a in range(1, copies):
            part = part + weights[:, a * HEAD_DIM : (a + 1) * HEAD_DIM]
        product = jnp.dot(
            weights.astype(jnp.bfloat16), held[1, span, :], preferred_element_type=jnp.float32
        )
        top_ref[...] = new_top
        total_ref[...] = part if start else total_ref[...] * factor + part
        o_ref[...] = product if start else o_ref[...] * factor + product

    def step(g, start):
        arrive(g)
        attend(own, g, start)
        arrive_prev(g)
        attend(prev, g, False)

    step(0, True)

    @pl.loop(1, N_ULY // GROUP)
    def _(g):
        step(g, False)

    diagonal = lax.broadcasted_iota(jnp.int32, (HEAD_DIM, HEAD_DIM), 0) == lax.broadcasted_iota(
        jnp.int32, (HEAD_DIM, HEAD_DIM), 1
    )
    for i in range(o_ref.shape[0] // HEAD_DIM):
        span = pl.ds(i * HEAD_DIM, HEAD_DIM)
        total = jnp.sum(total_ref[span, :], axis=1, keepdims=True)
        o_ref[span, :] = o_ref[span, :] / total
        logs = top_ref[span, :] * math.log(2) + jnp.log(total)
        l_ref[:, span] = jnp.sum(jnp.where(diagonal, logs, 0.0), axis=0, keepdims=True)

    @pl.loop(0, N_ULY)
    def _(j):
        @pl.when(j != OWN_SLOT)
        def _():
            send_q(j).wait_send()
            send_kv(j).wait_send()

        @pl.when(jnp.logical_not(last))
        def _():
            forward(j).wait_send()

        @pl.when(jnp.logical_and(last, lax.rem(j, N_Y) != N_Y - 1))
        def _():
            spread(j).wait_send()

    @pl.when(core == 1)
    def _():
        @pl.loop(0, N_ULY // N_Y)
        def _(k):
            cross_staged(k).wait_send()


def shards(qkv):
    tokens, _, width = qkv.shape
    block_len = tokens * N_ULY
    dma = pltpu.SemaphoreType.DMA
    return pl.pallas_call(
        kernel,
        name="regroup_attend",
        out_shape=(
            jax.ShapeDtypeStruct((block_len, HEAD_DIM), jnp.float32),
            jax.ShapeDtypeStruct((1, block_len), jnp.float32),
        ),
        in_specs=[pl.BlockSpec(memory_space=pl.ANY)],
        out_specs=(pl.BlockSpec(memory_space=pltpu.VMEM), pl.BlockSpec(memory_space=pltpu.VMEM)),
        scratch_shapes=[
            pltpu.VMEM((block_len, HEAD_DIM), jnp.bfloat16),
            pltpu.VMEM((2, block_len, HEAD_DIM), jnp.bfloat16),
            pltpu.VMEM((2, block_len, HEAD_DIM), jnp.bfloat16),
            pltpu.VMEM((N_ULY // N_Y, 2, tokens, HEAD_DIM), jnp.bfloat16),
            pltpu.VMEM((block_len, HEAD_DIM), jnp.float32),
            pltpu.VMEM((block_len, HEAD_DIM), jnp.float32),
            dma((2,)),
            dma((N_ULY,)), dma((N_ULY,)), dma((N_ULY,)), dma((N_ULY,)),
            dma((N_ULY,)), dma((N_ULY,)), dma((N_ULY,)),
            dma((N_ULY // N_Y,)), dma((N_ULY // N_Y,)),
        ],
        compiler_params=pltpu.CompilerParams(
            collective_id=0, has_side_effects=True, vmem_limit_bytes=48 << 20
        ),
        cost_estimate=pl.CostEstimate(
            flops=8 * block_len * block_len * HEAD_DIM,
            bytes_accessed=10 * block_len * HEAD_DIM,
            transcendentals=2 * block_len * block_len,
        ),
    )(jnp.transpose(qkv, (1, 0, 2)))


def solution(mesh):
    return jax.shard_map(
        shards,
        mesh=mesh,
        in_specs=(P(("blk", "uly"), None, None),),
        out_specs=(P("blk", "uly"), P("uly", "blk")),
        check_vma=False,
    )
```

time: 127 us -> 76.5 us (0.60)
  the two profiles are of different devices: /device:TPU:64 before, /device:TPU:49 now
where the time goes in v1:
time: 76.5 us; the launch traced here: 76.4 us
  Pallas kernels  73 us (95%)
  local copies, waits for them, and re-layouts  2.74 us (4%)
    pallas_call x1, Pallas kernels, shards(): pl.pallas_call(kernel, name='regroup_attend', out_shape=(jax.ShapeDtypeSt...  73 us
    unnamed x4, local copies, waits for them, and re-layouts  2.74 us

profile of v1, /device:TPU:49, one launch (start us, length us, event | category | flops | bytes accessed | tf_op | source)
XLA Modules:
  0.0 76.4 jit_solution(15456092815179730883)
XLA Ops:
  0.6 0.0 copy-start
  0.6 1.3 %copy-done = bf16[64,3,3072]{2,0,1:T(8,128)(2,1)S(1)} copy-done((bf16[64,3,3072]{2,0,1:T(8,128)(2,1)S(1)}, bf16[64,3,3072]{2,0,1:T(8,128)(2,1)}, u32[]{:S(2)}) %copy-start) | copy-done | bytes 1179672
  1.9 73.0 %regroup_attend.1 = (f32[1536,128]{1,0:T(8,128)S(1)}, f32[1,1536]{1,0:T(1,128)S(1)}) custom-call(bf16[3,64,3072]{2,1,0:T(8,128)(2,1)S(1)} %bitcast.1), custom_call_target="tpu_custom_call" | custom-call | flops 2415919104 | bytes 1966080 | tf_op jit(solution)/shard_map/regroup_attend/pallas_call | solution.py:270
  74.9 0.9 %copy.5 = f32[1536,128]{1,0:T(8,128)} copy(f32[1536,128]{1,0:T(8,128)S(1)} %get-tuple-element.4) | data formatting | bytes 1572864
  75.8 0.6 copy.6
Async XLA Ops:
  0.6 1.3 %copy-start = (bf16[64,3,3072]{2,0,1:T(8,128)(2,1)S(1)}, bf16[64,3,3072]{2,0,1:T(8,128)(2,1)}, u32[]{:S(2)}) copy-start(bf16[64,3,3072]{2,0,1:T(8,128)(2,1)} %param.1) | copy-start | bytes 3538948

commit v2 on v1

--- a/solution.py
+++ b/solution.py
@@ -16,6 +16,8 @@
 HALF = N_Z // 2
 OWN_SLOT = 1
 GROUP = 4
+N_RELAY = 12
+EARLY = 8
 SCALE = math.log2(math.e) / math.sqrt(HEAD_DIM)
 
 
@@ -32,7 +34,7 @@
 
 def kernel(
     x_ref, o_ref, l_ref, queries, own, prev, stage, top_ref, total_ref,
-    loc_sem, q_send, q_recv, kv_send, kv_recv, f_send, f_recv, a_send, a_recv, b_send,
+    loc_sem, q_send, q_recv, kv_send, kv_recv, f_send, f_recv, a_send, a_recv, b_send, ready,
 ):
     blk, uly = lax.axis_index("blk"), lax.axis_index("uly")
     zhi, y, core = blk // (2 * N_Y), lax.rem(blk // 2, N_Y), lax.rem(blk, 2)
@@ -40,13 +42,18 @@
     following, preceding = lax.rem(blk + 1, N_BLK), lax.rem(blk + N_BLK - 1, N_BLK)
     last = jnp.logical_and(y == N_Y - 1, core == 1)
     first = jnp.logical_and(y == 0, core == 0)
-    relay = jnp.logical_and(y != N_Y - 1, core == 1)
+    relay = jnp.logical_and(y >= 1, y <= N_RELAY // 2)
+    relay_slot = 2 * (2 * (y - 1) + core) + 1
 
     def block_at(zhi_, y_, core_):
         return (zhi_ * N_Y + y_) * 2 + core_
 
+    def relay_at(zhi_, c):
+        return block_at(zhi_, 1 + c // 2, lax.rem(c, 2))
+
     wrap_source = block_at(zhi, N_Y - 1, 1)
     wrap_target = block_at(1 - zhi, 0, 0)
+    wrap_origin = block_at(1 - zhi, N_Y - 1, 1)
 
     barrier = pltpu.get_barrier_semaphore()
 
@@ -64,17 +71,30 @@
     @pl.when(relay)
     def _():
         greet(wrap_source, uly)
-
-    @pl.when(first)
-    def _():
-        @pl.loop(0, N_ULY)
-        def _(j):
-            greet(block_at(1 - zhi, lax.rem(j, N_Y), 1), peer(uly, j, -1))
+        greet(wrap_target, peer(uly, relay_slot, 1))
+
+    @pl.when(last)
+    def _():
+        @pl.loop(0, N_RELAY)
+        def _(c):
+            greet(wrap_target, peer(uly, 2 * c, 1))
 
     pl.semaphore_wait(
         barrier,
-        N_ULY - 1 + jnp.where(last, N_Y - 1, 1) + jnp.where(core == 1, N_ULY // N_Y, 0),
+        N_ULY - 1 + jnp.where(last, N_RELAY, 1) + jnp.where(first, N_ULY, 0),
     )
+
+    @pl.when(first)
+    def _():
+        @pl.loop(0, N_RELAY)
+        def _(c):
+            pl.semaphore_signal(
+                ready, inc=1, device_id=(wrap_origin, peer(uly, 2 * c, -1)), device_id_type=MESH
+            )
+            pl.semaphore_signal(
+                ready, inc=1, device_id=(relay_at(1 - zhi, c), peer(uly, 2 * c + 1, -1)),
+                device_id_type=MESH,
+            )
 
     def rows(s):
         return pl.ds(pl.multiple_of(s * tokens, tokens), tokens)
@@ -104,24 +124,22 @@
             device_id=(following, uly),
         )
 
-    def spread(j):
-        return remote(
-            x_ref.at[1:3, :, head(peer(uly, j, 1))], stage.at[j // N_Y], a_send.at[j],
-            a_recv.at[j // N_Y], device_id=(block_at(zhi, lax.rem(j, N_Y), 1), uly),
-        )
-
-    def cross_staged(k):
-        j = k * N_Y + y
-        return remote(
-            stage.at[k], prev.at[:, rows(j)], b_send.at[k], f_recv.at[j],
-            device_id=(wrap_target, peer(uly, j, 1)),
-        )
-
-    def cross_direct(k):
-        j = k * N_Y + N_Y - 1
-        to = peer(uly, j, 1)
-        return remote(
-            x_ref.at[1:3, :, head(to)], prev.at[:, rows(j)], b_send.at[k], f_recv.at[j],
+    def spread(c):
+        return remote(
+            x_ref.at[1:3, :, head(peer(uly, 2 * c + 1, 1))], stage, a_send.at[c], a_recv,
+            device_id=(relay_at(zhi, c), uly),
+        )
+
+    def cross_staged():
+        return remote(
+            stage, prev.at[:, rows(relay_slot)], b_send.at[0], f_recv.at[relay_slot],
+            device_id=(wrap_target, peer(uly, relay_slot, 1)),
+        )
+
+    def cross_direct(c):
+        to = peer(uly, 2 * c, 1)
+        return remote(
+            x_ref.at[1:3, :, head(to)], prev.at[:, rows(2 * c)], b_send.at[c], f_recv.at[2 * c],
             device_id=(wrap_target, to),
         )
 
@@ -132,34 +150,43 @@
     own_q.start()
     own_kv.start()
 
+    @pl.when(last)
+    def _():
+        @pl.loop(0, N_RELAY)
+        def _(c):
+            spread(c).start()
+
     @pl.loop(0, N_ULY)
     def _(j):
         @pl.when(j != OWN_SLOT)
         def _():
             send_q(j).start()
 
-        @pl.when(jnp.logical_and(last, lax.rem(j, N_Y) != N_Y - 1))
-        def _():
-            spread(j).start()
+    @pl.loop(0, EARLY)
+    def _(j):
+        @pl.when(j != OWN_SLOT)
+        def _():
+            send_kv(j).start()
 
     @pl.when(relay)
     def _():
-        @pl.loop(0, N_ULY // N_Y)
-        def _(k):
-            spread(k * N_Y).wait_recv()
-            cross_staged(k).start()
+        pl.semaphore_wait(ready, 1)
+        spread(0).wait_recv()
+        cross_staged().start()
 
     @pl.when(last)
     def _():
-        @pl.loop(0, N_ULY // N_Y)
-        def _(k):
-            cross_direct(k).start()
-
-    @pl.loop(0, N_ULY)
-    def _(j):
-        @pl.when(j != OWN_SLOT)
-        def _():
-            send_kv(j).start()
+        pl.semaphore_wait(ready, N_RELAY)
+
+    @pl.loop(EARLY, N_ULY)
+    def _(j):
+        @pl.when(last)
+        def _():
+            @pl.when(j < EARLY + N_RELAY)
+            def _():
+                cross_direct(j - EARLY).start()
+
+        send_kv(j).start()
 
     own_q.wait()
     own_kv.wait()
@@ -219,17 +246,27 @@
         total_ref[...] = part if start else total_ref[...] * factor + part
         o_ref[...] = product if start else o_ref[...] * factor + product
 
-    def step(g, start):
+    groups = N_ULY // GROUP
+    lag = 2
+    arrive(0)
+    attend(own, 0, True)
+
+    def take_own(g):
         arrive(g)
-        attend(own, g, start)
+        attend(own, g, False)
+
+    def take_prev(g):
         arrive_prev(g)
         attend(prev, g, False)
 
-    step(0, True)
-
-    @pl.loop(1, N_ULY // GROUP)
+    pl.loop(1, lag)(take_own)
+
+    @pl.loop(lag, groups)
     def _(g):
-        step(g, False)
+        take_own(g)
+        take_prev(g - lag)
+
+    pl.loop(groups - lag, groups)(take_prev)
 
     diagonal = lax.broadcasted_iota(jnp.int32, (HEAD_DIM, HEAD_DIM), 0) == lax.broadcasted_iota(
         jnp.int32, (HEAD_DIM, HEAD_DIM), 1
@@ -252,15 +289,16 @@
         def _():
             forward(j).wait_send()
 
-        @pl.when(jnp.logical_and(last, lax.rem(j, N_Y) != N_Y - 1))
-        def _():
-            spread(j).wait_send()
-
-    @pl.when(core == 1)
-    def _():
-        @pl.loop(0, N_ULY // N_Y)
-        def _(k):
-            cross_staged(k).wait_send()
+    @pl.when(last)
+    def _():
+        @pl.loop(0, N_RELAY)
+        def _(c):
+            spread(c).wait_send()
+            cross_direct(c).wait_send()
+
+    @pl.when(relay)
+    def _():
+        cross_staged().wait_send()
 
 
 def shards(qkv):
@@ -274,19 +312,19 @@
             jax.ShapeDtypeStruct((block_len, HEAD_DIM), jnp.float32),
             jax.ShapeDtypeStruct((1, block_len), jnp.float32),
         ),
-        in_specs=[pl.BlockSpec(memory_space=pl.ANY)],
+        in_specs=[pl.BlockSpec(memory_space=pltpu.HBM)],
         out_specs=(pl.BlockSpec(memory_space=pltpu.VMEM), pl.BlockSpec(memory_space=pltpu.VMEM)),
         scratch_shapes=[
             pltpu.VMEM((block_len, HEAD_DIM), jnp.bfloat16),
             pltpu.VMEM((2, block_len, HEAD_DIM), jnp.bfloat16),
             pltpu.VMEM((2, block_len, HEAD_DIM), jnp.bfloat16),
-            pltpu.VMEM((N_ULY // N_Y, 2, tokens, HEAD_DIM), jnp.bfloat16),
+            pltpu.VMEM((2, tokens, HEAD_DIM), jnp.bfloat16),
             pltpu.VMEM((block_len, HEAD_DIM), jnp.float32),
             pltpu.VMEM((block_len, HEAD_DIM), jnp.float32),
             dma((2,)),
             dma((N_ULY,)), dma((N_ULY,)), dma((N_ULY,)), dma((N_ULY,)),
-            dma((N_ULY,)), dma((N_ULY,)), dma((N_ULY,)),
-            dma((N_ULY // N_Y,)), dma((N_ULY // N_Y,)),
+            dma((N_ULY,)), dma((N_ULY,)), dma((N_RELAY,)), dma, dma((N_RELAY,)),
+            pltpu.SemaphoreType.REGULAR,
         ],
         compiler_params=pltpu.CompilerParams(
             collective_id=0, has_side_effects=True, vmem_limit_bytes=48 << 20

time: 76.5 us -> 65.5 us (0.86)
  the two profiles are of different devices: /device:TPU:49 before, /device:TPU:104 now
where the time goes in v2:
time: 65.5 us; the launch traced here: 65.3 us
  Pallas kernels  61.9 us (95%)
  local copies, waits for them, and re-layouts  2.74 us (4%)
    pallas_call x1, Pallas kernels, shards(): pl.pallas_call(kernel, name='regroup_attend', out_shape=(jax.ShapeDtypeSt...  61.9 us
    unnamed x4, local copies, waits for them, and re-layouts  2.74 us

profile of v2, /device:TPU:104, one launch (start us, length us, event | category | flops | bytes accessed | tf_op | source)
XLA Modules:
  0.0 65.3 jit_solution(16513102705745404579)
XLA Ops:
  0.6 0.0 copy-start
  0.6 1.3 %copy-done = bf16[64,3,3072]{2,0,1:T(8,128)(2,1)S(1)} copy-done((bf16[64,3,3072]{2,0,1:T(8,128)(2,1)S(1)}, bf16[64,3,3072]{2,0,1:T(8,128)(2,1)}, u32[]{:S(2)}) %copy-start) | copy-done | bytes 1179672
  1.9 61.9 %regroup_attend.1 = (f32[1536,128]{1,0:T(8,128)S(1)}, f32[1,1536]{1,0:T(1,128)S(1)}) custom-call(bf16[3,64,3072]{2,1,0:T(8,128)(2,1)S(1)} %bitcast.1), custom_call_target="tpu_custom_call" | custom-call | flops 2415919104 | bytes 1966080 | tf_op jit(solution)/shard_map/regroup_attend/pallas_call | solution.py:308
  63.8 0.9 %copy.5 = f32[1536,128]{1,0:T(8,128)} copy(f32[1536,128]{1,0:T(8,128)S(1)} %get-tuple-element.4) | data formatting | bytes 1572864
  64.7 0.6 copy.6
Async XLA Ops:
  0.6 1.3 %copy-start = (bf16[64,3,3072]{2,0,1:T(8,128)(2,1)S(1)}, bf16[64,3,3072]{2,0,1:T(8,128)(2,1)}, u32[]{:S(2)}) copy-start(bf16[64,3,3072]{2,0,1:T(8,128)(2,1)} %param.1) | copy-start | bytes 3538948

commit v3 on v2

--- a/solution.py
+++ b/solution.py
@@ -33,7 +33,7 @@
 
 
 def kernel(
-    x_ref, o_ref, l_ref, queries, own, prev, stage, top_ref, total_ref,
+    x_ref, o_ref, top_ref, total_ref, queries, own, prev, stage,
     loc_sem, q_send, q_recv, kv_send, kv_recv, f_send, f_recv, a_send, a_recv, b_send, ready,
 ):
     blk, uly = lax.axis_index("blk"), lax.axis_index("uly")
@@ -43,6 +43,7 @@
     last = jnp.logical_and(y == N_Y - 1, core == 1)
     first = jnp.logical_and(y == 0, core == 0)
     relay = jnp.logical_and(y >= 1, y <= N_RELAY // 2)
+    lower = zhi == 0
     relay_slot = 2 * (2 * (y - 1) + core) + 1
 
     def block_at(zhi_, y_, core_):
@@ -71,20 +72,30 @@
     @pl.when(relay)
     def _():
         greet(wrap_source, uly)
+
+    @pl.when(jnp.logical_and(relay, lower))
+    def _():
         greet(wrap_target, peer(uly, relay_slot, 1))
 
-    @pl.when(last)
+    @pl.when(jnp.logical_and(last, lower))
     def _():
         @pl.loop(0, N_RELAY)
         def _(c):
             greet(wrap_target, peer(uly, 2 * c, 1))
 
-    pl.semaphore_wait(
-        barrier,
-        N_ULY - 1 + jnp.where(last, N_RELAY, 1) + jnp.where(first, N_ULY, 0),
+    @pl.when(jnp.logical_and(first, lower))
+    def _():
+        @pl.loop(0, N_RELAY)
+        def _(c):
+            greet(wrap_origin, peer(uly, 2 * c, -1))
+            greet(relay_at(1 - zhi, c), peer(uly, 2 * c + 1, -1))
+
+    extra = jnp.where(
+        lower, 0, jnp.where(first, N_ULY, jnp.where(last, N_RELAY, jnp.where(relay, 1, 0)))
     )
-
-    @pl.when(first)
+    pl.semaphore_wait(barrier, N_ULY - 1 + jnp.where(last, N_RELAY, 1) + extra)
+
+    @pl.when(jnp.logical_and(first, jnp.logical_not(lower)))
     def _():
         @pl.loop(0, N_RELAY)
         def _(c):
@@ -170,11 +181,14 @@
 
     @pl.when(relay)
     def _():
-        pl.semaphore_wait(ready, 1)
+        @pl.when(lower)
+        def _():
+            pl.semaphore_wait(ready, 1)
+
         spread(0).wait_recv()
         cross_staged().start()
 
-    @pl.when(last)
+    @pl.when(jnp.logical_and(last, lower))
     def _():
         pl.semaphore_wait(ready, N_RELAY)
 
@@ -247,7 +261,7 @@
         o_ref[...] = product if start else o_ref[...] * factor + product
 
     groups = N_ULY // GROUP
-    lag = 2
+    lag = 3
     arrive(0)
     attend(own, 0, True)
 
@@ -261,66 +275,67 @@
 
     pl.loop(1, lag)(take_own)
 
-    @pl.loop(lag, groups)
+    @pl.loop(lag, groups - 1)
     def _(g):
         take_own(g)
         take_prev(g - lag)
 
+    take_prev(groups - 1 - lag)
+    take_own(groups - 1)
     pl.loop(groups - lag, groups)(take_prev)
 
+    @pl.loop(0, N_ULY)
+    def _(j):
+        @pl.when(j != OWN_SLOT)
+        def _():
+            send_q(j).wait_send()
+            send_kv(j).wait_send()
+
+        @pl.when(jnp.logical_not(last))
+        def _():
+            forward(j).wait_send()
+
+    @pl.when(last)
+    def _():
+        @pl.loop(0, N_RELAY)
+        def _(c):
+            spread(c).wait_send()
+            cross_direct(c).wait_send()
+
+    @pl.when(relay)
+    def _():
+        cross_staged().wait_send()
+
+
+def finish(a_ref, top_ref, total_ref, o_ref, l_ref):
     diagonal = lax.broadcasted_iota(jnp.int32, (HEAD_DIM, HEAD_DIM), 0) == lax.broadcasted_iota(
         jnp.int32, (HEAD_DIM, HEAD_DIM), 1
     )
     for i in range(o_ref.shape[0] // HEAD_DIM):
         span = pl.ds(i * HEAD_DIM, HEAD_DIM)
         total = jnp.sum(total_ref[span, :], axis=1, keepdims=True)
-        o_ref[span, :] = o_ref[span, :] / total
+        o_ref[span, :] = a_ref[span, :] / total
         logs = top_ref[span, :] * math.log(2) + jnp.log(total)
         l_ref[:, span] = jnp.sum(jnp.where(diagonal, logs, 0.0), axis=0, keepdims=True)
-
-    @pl.loop(0, N_ULY)
-    def _(j):
-        @pl.when(j != OWN_SLOT)
-        def _():
-            send_q(j).wait_send()
-            send_kv(j).wait_send()
-
-        @pl.when(jnp.logical_not(last))
-        def _():
-            forward(j).wait_send()
-
-    @pl.when(last)
-    def _():
-        @pl.loop(0, N_RELAY)
-        def _(c):
-            spread(c).wait_send()
-            cross_direct(c).wait_send()
-
-    @pl.when(relay)
-    def _():
-        cross_staged().wait_send()
 
 
 def shards(qkv):
     tokens, _, width = qkv.shape
     block_len = tokens * N_ULY
     dma = pltpu.SemaphoreType.DMA
-    return pl.pallas_call(
+    in_vmem = pl.BlockSpec(memory_space=pltpu.VMEM)
+    rows = jax.ShapeDtypeStruct((block_len, HEAD_DIM), jnp.float32)
+    parts = pl.pallas_call(
         kernel,
         name="regroup_attend",
-        out_shape=(
-            jax.ShapeDtypeStruct((block_len, HEAD_DIM), jnp.float32),
-            jax.ShapeDtypeStruct((1, block_len), jnp.float32),
-        ),
+        out_shape=(rows, rows, rows),
         in_specs=[pl.BlockSpec(memory_space=pltpu.HBM)],
-        out_specs=(pl.BlockSpec(memory_space=pltpu.VMEM), pl.BlockSpec(memory_space=pltpu.VMEM)),
+        out_specs=(in_vmem, in_vmem, in_vmem),
         scratch_shapes=[
             pltpu.VMEM((block_len, HEAD_DIM), jnp.bfloat16),
             pltpu.VMEM((2, block_len, HEAD_DIM), jnp.bfloat16),
             pltpu.VMEM((2, block_len, HEAD_DIM), jnp.bfloat16),
             pltpu.VMEM((2, tokens, HEAD_DIM), jnp.bfloat16),
-            pltpu.VMEM((block_len, HEAD_DIM), jnp.float32),
-            pltpu.VMEM((block_len, HEAD_DIM), jnp.float32),
             dma((2,)),
             dma((N_ULY,)), dma((N_ULY,)), dma((N_ULY,)), dma((N_ULY,)),
             dma((N_ULY,)), dma((N_ULY,)), dma((N_RELAY,)), dma, dma((N_RELAY,)),
@@ -334,7 +349,15 @@
             bytes_accessed=10 * block_len * HEAD_DIM,
             transcendentals=2 * block_len * block_len,
         ),
-    )(jnp.transpose(qkv, (1, 0, 2)))
+    )(pltpu.with_memory_space_constraint(jnp.transpose(qkv, (1, 0, 2)), pltpu.HBM))
+    return pl.pallas_call(
+        finish,
+        name="finish",
+        out_shape=(rows, jax.ShapeDtypeStruct((1, block_len), jnp.float32)),
+        in_specs=[in_vmem] * 3,
+        out_specs=(in_vmem, in_vmem),
+        compiler_params=pltpu.CompilerParams(vmem_limit_bytes=8 << 20),
+    )(*parts)
 
 
 def solution(mesh):

time: 65.5 us -> 63.7 us (0.973)
  local copies, waits for them, and re-layouts: 2.74 us -> 0 us
  Pallas kernels: 61.9 us -> 63 us
    unnamed x4 -> x0, local copies, waits for them, and re-layouts: 2.74 us -> none
    pallas_call x1 -> x2, Pallas kernels: 61.9 us -> 63 us  [the longest x1 61.8 us: shards(): pl.pallas_call(kernel, name='regroup_attend', out_shape=(rows, rows, rows...]
where the time goes in v3:
time: 63.7 us; the launch traced here: 63.6 us
  Pallas kernels  63 us (99%)
  between operations  0.64 us (1%)
    pallas_call x1, Pallas kernels, shards(): pl.pallas_call(kernel, name='regroup_attend', out_shape=(rows, rows, rows...  61.8 us

profile of v3, /device:TPU:104, one launch (start us, length us, event | category | flops | bytes accessed | tf_op | source)
XLA Modules:
  0.0 63.6 jit_solution(16764392996497428374)
XLA Ops:
  0.6 61.8 %regroup_attend.1 = (f32[1536,128]{1,0:T(8,128)S(1)}, f32[1536,128]{1,0:T(8,128)S(1)}, f32[1536,128]{1,0:T(8,128)S(1)}) custom-call(bf16[3,64,3072]{2,1,0:T(8,128)(2,1)} %bitcast.1), custom_call_target="tpu_custom_call" | custom-call | flops 2415919104 | bytes 1966080 | tf_op jit(solution)/shard_map/regroup_attend/pallas_call | solution.py:328
  62.4 1.2 %finish.1 = (f32[1536,128]{1,0:T(8,128)}, f32[1,1536]{1,0:T(1,128)}) custom-call(f32[1536,128]{1,0:T(8,128)S(1)} %get-tuple-element.5.a_ref, f32[1536,128]{1,0:T(8,128)S(1)} %get-tuple-element.6.top_ref, f32[1536,128]{1,0:T(8,128)S(1)} %get-tuple-element.7.total_ref), custom_call_target="tpu_custom_call" | custom-call | tf_op jit(solution)/shard_map/finish/pallas_call | solution.py:353

commit v4 on v3

--- a/solution.py
+++ b/solution.py
@@ -14,17 +14,17 @@
 N_ULY = N_X * N_Z
 N_BLK = 32
 HALF = N_Z // 2
-OWN_SLOT = 1
+OWN_SLOT = 0
 GROUP = 4
 N_RELAY = 12
-EARLY = 8
+EARLY = 4
 SCALE = math.log2(math.e) / math.sqrt(HEAD_DIM)
 
 
 def peer(uly, slot, sign):
     x, z = uly // N_Z, lax.rem(uly, N_Z)
     half, place = z // HALF, lax.rem(z, HALF)
-    near, turn = lax.rem(slot, 2), slot // 2
+    near, turn = 1 - slot // 12, lax.rem(slot, 12)
     dz, dx = turn // N_X, lax.rem(turn, N_X)
     to_half = jnp.where(near == 1, half, 1 - half)
     to_place = lax.rem(place + sign * dz + HALF, HALF)
@@ -44,7 +44,7 @@
     first = jnp.logical_and(y == 0, core == 0)
     relay = jnp.logical_and(y >= 1, y <= N_RELAY // 2)
     lower = zhi == 0
-    relay_slot = 2 * (2 * (y - 1) + core) + 1
+    relay_slot = 2 * (y - 1) + core + 0
 
     def block_at(zhi_, y_, core_):
         return (zhi_ * N_Y + y_) * 2 + core_
@@ -81,14 +81,14 @@
     def _():
         @pl.loop(0, N_RELAY)
         def _(c):
-            greet(wrap_target, peer(uly, 2 * c, 1))
+            greet(wrap_target, peer(uly, c + 12, 1))
 
     @pl.when(jnp.logical_and(first, lower))
     def _():
         @pl.loop(0, N_RELAY)
         def _(c):
-            greet(wrap_origin, peer(uly, 2 * c, -1))
-            greet(relay_at(1 - zhi, c), peer(uly, 2 * c + 1, -1))
+            greet(wrap_origin, peer(uly, c + 12, -1))
+            greet(relay_at(1 - zhi, c), peer(uly, (c + 0), -1))
 
     extra = jnp.where(
         lower, 0, jnp.where(first, N_ULY, jnp.where(last, N_RELAY, jnp.where(relay, 1, 0)))
@@ -100,10 +100,10 @@
         @pl.loop(0, N_RELAY)
         def _(c):
             pl.semaphore_signal(
-                ready, inc=1, device_id=(wrap_origin, peer(uly, 2 * c, -1)), device_id_type=MESH
+                ready, inc=1, device_id=(wrap_origin, peer(uly, c + 12, -1)), device_id_type=MESH
             )
             pl.semaphore_signal(
-                ready, inc=1, device_id=(relay_at(1 - zhi, c), peer(uly, 2 * c + 1, -1)),
+                ready, inc=1, device_id=(relay_at(1 - zhi, c), peer(uly, (c + 0), -1)),
                 device_id_type=MESH,
             )
 
@@ -137,7 +137,7 @@
 
     def spread(c):
         return remote(
-            x_ref.at[1:3, :, head(peer(uly, 2 * c + 1, 1))], stage, a_send.at[c], a_recv,
+            x_ref.at[1:3, :, head(peer(uly, (c + 0), 1))], stage, a_send.at[c], a_recv,
             device_id=(relay_at(zhi, c), uly),
         )
 
@@ -148,9 +148,9 @@
         )
 
     def cross_direct(c):
-        to = peer(uly, 2 * c, 1)
-        return remote(
-            x_ref.at[1:3, :, head(to)], prev.at[:, rows(2 * c)], b_send.at[c], f_recv.at[2 * c],
+        to = peer(uly, c + 12, 1)
+        return remote(
+            x_ref.at[1:3, :, head(to)], prev.at[:, rows((c + 12))], b_send.at[c], f_recv.at[c + 12],
             device_id=(wrap_target, to),
         )
 
@@ -167,8 +167,16 @@
         def _(c):
             spread(c).start()
 
+    @pl.when(jnp.logical_and(last, jnp.logical_not(lower)))
+    def _():
+        @pl.loop(0, N_RELAY)
+        def _(c):
+            cross_direct(c).start()
+
     @pl.loop(0, N_ULY)
-    def _(j):
+    def _(i):
+        j = lax.rem(i + N_ULY // 2, N_ULY)
+
         @pl.when(j != OWN_SLOT)
         def _():
             send_q(j).start()
@@ -194,13 +202,15 @@
 
     @pl.loop(EARLY, N_ULY)
     def _(j):
-        @pl.when(last)
+        @pl.when(jnp.logical_and(last, lower))
         def _():
             @pl.when(j < EARLY + N_RELAY)
             def _():
                 cross_direct(j - EARLY).start()
 
-        send_kv(j).start()
+        @pl.when(j != OWN_SLOT)
+        def _():
+            send_kv(j).start()
 
     own_q.wait()
     own_kv.wait()
@@ -261,7 +271,7 @@
         o_ref[...] = product if start else o_ref[...] * factor + product
 
     groups = N_ULY // GROUP
-    lag = 3
+    lag = 2
     arrive(0)
     attend(own, 0, True)
 

time: 63.7 us -> 62.1 us (0.975)
  Pallas kernels: 63 us -> 61.4 us
    pallas_call x1, Pallas kernels: 61.8 us -> 60.2 us  [shards(): pl.pallas_call(kernel, name='regroup_attend', out_shape=(rows, rows, rows...]
where the time goes in v4:
time: 62.1 us; the launch traced here: 62 us
  Pallas kernels  61.4 us (99%)
  between operations  0.64 us (1%)
    pallas_call x1, Pallas kernels, shards(): pl.pallas_call(kernel, name='regroup_attend', out_shape=(rows, rows, rows...  60.2 us

profile of v4, /device:TPU:104, one launch (start us, length us, event | category | flops | bytes accessed | tf_op | source)
XLA Modules:
  0.0 62.0 jit_solution(15074768167503309288)
XLA Ops:
  0.6 60.2 %regroup_attend.1 = (f32[1536,128]{1,0:T(8,128)S(1)}, f32[1536,128]{1,0:T(8,128)S(1)}, f32[1536,128]{1,0:T(8,128)S(1)}) custom-call(bf16[3,64,3072]{2,1,0:T(8,128)(2,1)} %bitcast.1), custom_call_target="tpu_custom_call" | custom-call | flops 2415919104 | bytes 1966080 | tf_op jit(solution)/shard_map/regroup_attend/pallas_call | solution.py:338
  60.8 1.2 %finish.1 = (f32[1536,128]{1,0:T(8,128)}, f32[1,1536]{1,0:T(1,128)}) custom-call(f32[1536,128]{1,0:T(8,128)S(1)} %get-tuple-element.5.a_ref, f32[1536,128]{1,0:T(8,128)S(1)} %get-tuple-element.6.top_ref, f32[1536,128]{1,0:T(8,128)S(1)} %get-tuple-element.7.total_ref), custom_call_target="tpu_custom_call" | custom-call | tf_op jit(solution)/shard_map/finish/pallas_call | solution.py:363

commit v5 on v4

--- a/solution.py
+++ b/solution.py
@@ -17,7 +17,7 @@
 OWN_SLOT = 0
 GROUP = 4
 N_RELAY = 12
-EARLY = 4
+EARLY = 12
 SCALE = math.log2(math.e) / math.sqrt(HEAD_DIM)
 
 

time: 62.1 us -> 63.4 us (1.021)
  the two profiles are of different devices: /device:TPU:104 before, /device:TPU:1 now
where the time goes in v5:
time: 63.4 us; the launch traced here: 63.3 us
  Pallas kernels  62.7 us (99%)
  between operations  0.64 us (1%)
    pallas_call x1, Pallas kernels, shards(): pl.pallas_call(kernel, name='regroup_attend', out_shape=(rows, rows, rows...  61.5 us

profile of v5, /device:TPU:1, one launch (start us, length us, event | category | flops | bytes accessed | tf_op | source)
XLA Modules:
  0.0 63.3 jit_solution(13831148438932476822)
XLA Ops:
  0.6 61.5 %regroup_attend.1 = (f32[1536,128]{1,0:T(8,128)S(1)}, f32[1536,128]{1,0:T(8,128)S(1)}, f32[1536,128]{1,0:T(8,128)S(1)}) custom-call(bf16[3,64,3072]{2,1,0:T(8,128)(2,1)} %bitcast.1), custom_call_target="tpu_custom_call" | custom-call | flops 2415919104 | bytes 1966080 | tf_op jit(solution)/shard_map/regroup_attend/pallas_call | solution.py:338
  62.1 1.2 %finish.1 = (f32[1536,128]{1,0:T(8,128)}, f32[1,1536]{1,0:T(1,128)}) custom-call(f32[1536,128]{1,0:T(8,128)S(1)} %get-tuple-element.5.a_ref, f32[1536,128]{1,0:T(8,128)S(1)} %get-tuple-element.6.top_ref, f32[1536,128]{1,0:T(8,128)S(1)} %get-tuple-element.7.total_ref), custom_call_target="tpu_custom_call" | custom-call | tf_op jit(solution)/shard_map/finish/pallas_call | solution.py:363

commit v6 on v5

--- a/solution.py
+++ b/solution.py
@@ -17,7 +17,7 @@
 OWN_SLOT = 0
 GROUP = 4
 N_RELAY = 12
-EARLY = 12
+EARLY = 1
 SCALE = math.log2(math.e) / math.sqrt(HEAD_DIM)
 
 

time: 63.4 us -> 62.1 us (0.979)
  the two profiles are of different devices: /device:TPU:1 before, /device:TPU:104 now
where the time goes in v6:
time: 62.1 us; the launch traced here: 62 us
  Pallas kernels  61.4 us (99%)
  between operations  0.64 us (1%)
    pallas_call x1, Pallas kernels, shards(): pl.pallas_call(kernel, name='regroup_attend', out_shape=(rows, rows, rows...  60.2 us

profile of v6, /device:TPU:104, one launch (start us, length us, event | category | flops | bytes accessed | tf_op | source)
XLA Modules:
  0.0 62.0 jit_solution(18136945991658047494)
XLA Ops:
  0.6 60.2 %regroup_attend.1 = (f32[1536,128]{1,0:T(8,128)S(1)}, f32[1536,128]{1,0:T(8,128)S(1)}, f32[1536,128]{1,0:T(8,128)S(1)}) custom-call(bf16[3,64,3072]{2,1,0:T(8,128)(2,1)} %bitcast.1), custom_call_target="tpu_custom_call" | custom-call | flops 2415919104 | bytes 1966080 | tf_op jit(solution)/shard_map/regroup_attend/pallas_call | solution.py:338
  60.8 1.2 %finish.1 = (f32[1536,128]{1,0:T(8,128)}, f32[1,1536]{1,0:T(1,128)}) custom-call(f32[1536,128]{1,0:T(8,128)S(1)} %get-tuple-element.5.a_ref, f32[1536,128]{1,0:T(8,128)S(1)} %get-tuple-element.6.top_ref, f32[1536,128]{1,0:T(8,128)S(1)} %get-tuple-element.7.total_ref), custom_call_target="tpu_custom_call" | custom-call | tf_op jit(solution)/shard_map/finish/pallas_call | solution.py:363
